TPU v7x, 32 devices: a whole 2x2x4 slice. The times are simulated.
32 devices in a mesh: qry: 8 (over z, core), lib: 4 (over y, x).
Axes of the slice: x: 2, y: 2, z: 4, core: 2. Of those that a mesh axis runs over, the one named last changes fastest.
Arguments:
- query_prints: bfloat16 [256, 2048], P('qry'), may hold values from -500 to 500, as said below
- library_prints: bfloat16 [24576, 2048], P(('lib', 'qry')), may hold values from -1500 to 1500
- query_atoms: float32 [256, 192], P(('qry', 'lib')), may hold values from -3 to 3, as said below
- conformer_atoms: float32 [24576, 192], P(('lib', 'qry')), may hold values from -3 to 3, as said below
- candidates: int32 [256, 64], P(('qry', 'lib')), may hold values from 0 to 24575, as said below
- candidate_count: int32 [256], P(('qry', 'lib')), may hold values from 16 to 64
- home_row: int32 [24576], replicated, may hold values from 0 to 24575, as said below
Outputs:
- tversky: bfloat16 [256, 24576], P(None, ('lib', 'qry'))
- rescore: float32 [256, 64], P(('qry', 'lib'))
Inputs may be any that keep to these rules, and one draw needn't show every extreme that they name: query_prints rows and columns carry independent positive scales. `query_atoms`: each row holds x, y and z of 48 atom slots, then their weights; a padded slot has weight 0, and every row has at least one atom of positive weight. `conformer_atoms`: each row holds x, y and z of 48 atom slots, then their weights; a padded slot has weight 0, and every row has at least one atom of positive weight. Among the candidates in the rows of one device (8 queries, padding included), at most 36 have storage rows in any one block of rows b * 768 to (b + 1) * 768 - 1; in every draw some such block receives exactly 36 from the rows of every device. `home_row`: a permutation of 0 to 24575.
All inputs are finite; a program needn't handle non-finite values.
Results may differ from a plain program's by a relative error of at most 0.0029.
Values may be sent and summed in bfloat16 or wider, within the bound.
A program may use at most 64 MiB of HBM per device.

v0:
```python
import jax
import jax.numpy as jnp
from jax import lax
from jax.sharding import PartitionSpec as P

SHARPNESS = 0.8
EPSILON = 1e-06


def screen_rows(piece, library):
    scores = lax.dot_general(
        piece, library, (((1,), (1,)), ((), ())), preferred_element_type=jnp.float32
    )
    norms = jnp.sum(jnp.square(piece.astype(jnp.float32)), axis=1, keepdims=True)
    return (scores / (norms + EPSILON)).astype(jnp.bfloat16)


def selector(indices, rows):
    return (jnp.arange(rows, dtype=jnp.int32)[:, None] == indices[None, :]).astype(jnp.float32)


def pick_columns(table, indices):
    picks = selector(indices, table.shape[0])
    columns = lax.dot_general(
        table,
        picks,
        (((0,), (0,)), ((), ())),
        precision=lax.Precision.HIGHEST,
        preferred_element_type=jnp.float32,
    )
    return columns.reshape(4, -1, indices.shape[0])


def pick_rows(table, indices):
    picks = selector(indices, table.shape[0])
    return lax.dot_general(
        picks,
        table,
        (((0,), (0,)), ((), ())),
        precision=lax.Precision.HIGHEST,
        preferred_element_type=jnp.float32,
    )


def to_atoms(flat):
    return flat.reshape(flat.shape[0], 4, -1).transpose(1, 2, 0)


def intersection(first, second):
    dist = jnp.square(first[0][:, None, :] - second[0][None, :, :])
    dist = dist + jnp.square(first[1][:, None, :] - second[1][None, :, :])
    dist = dist + jnp.square(first[2][:, None, :] - second[2][None, :, :])
    return jnp.sum(
        first[3][:, None, :] * second[3][None, :, :] * jnp.exp(-SHARPNESS * dist), axis=(0, 1)
    )


def body(
    query_prints,
    library_prints,
    query_atoms,
    conformer_atoms,
    candidates,
    candidate_count,
    home_row,
):
    query_groups = lax.axis_size("qry")
    library_groups = lax.axis_size("lib")
    devices = query_groups * library_groups
    own_rows = library_prints.shape[0]
    local_queries = query_atoms.shape[0]
    listed = candidates.shape[1]
    pairs = local_queries * listed
    capacity = 2 * ((pairs + devices - 1) // devices) + 4
    tversky = screen_rows(lax.all_gather(query_prints, "qry", axis=0, tiled=True), library_prints)
    stored = jnp.take(home_row, candidates.reshape(-1), axis=0)
    owner = stored // own_rows
    slot_index = stored - owner * own_rows
    first_query = (lax.axis_index("qry") * library_groups + lax.axis_index("lib")) * local_queries
    query_index = first_query + jnp.arange(pairs, dtype=jnp.int32) // listed
    position = jnp.arange(pairs, dtype=jnp.int32)
    earlier = position[:, None] > position[None, :]
    same_owner = owner[:, None] == owner[None, :]
    rank = jnp.sum((earlier & same_owner).astype(jnp.int32), axis=1)
    target = owner * capacity + rank
    bucket_shape = (library_groups, query_groups, capacity)
    send_slot = (
        jnp.zeros(devices * capacity, jnp.int32).at[target].set(slot_index).reshape(bucket_shape)
    )
    send_query = (
        jnp.zeros(devices * capacity, jnp.int32).at[target].set(query_index).reshape(bucket_shape)
    )
    got_slot, got_query = (
        lax.all_to_all(
            lax.all_to_all(send_slot, "qry", split_axis=1, concat_axis=1, tiled=True),
            "lib",
            split_axis=0,
            concat_axis=0,
            tiled=True,
        ),
        lax.all_to_all(
            lax.all_to_all(send_query, "qry", split_axis=1, concat_axis=1, tiled=True),
            "lib",
            split_axis=0,
            concat_axis=0,
            tiled=True,
        ),
    )
    flat_slots = got_slot.reshape(-1)
    fetched = pick_rows(conformer_atoms, flat_slots).reshape(
        library_groups, query_groups, capacity, -1
    )
    prior_all = tversky[got_query.reshape(-1), flat_slots].astype(jnp.float32).reshape(bucket_shape)
    back_atoms, back_prior = (
        lax.all_to_all(
            lax.all_to_all(
                fetched.astype(jnp.bfloat16), "qry", split_axis=1, concat_axis=1, tiled=True
            ),
            "lib",
            split_axis=0,
            concat_axis=0,
            tiled=True,
        ).astype(fetched.dtype),
        lax.all_to_all(
            lax.all_to_all(
                prior_all.astype(jnp.bfloat16), "qry", split_axis=1, concat_axis=1, tiled=True
            ),
            "lib",
            split_axis=0,
            concat_axis=0,
            tiled=True,
        ).astype(prior_all.dtype),
    )
    conformer = pick_columns(back_atoms.reshape(devices * capacity, -1), target)
    fragment = jnp.repeat(to_atoms(query_atoms), listed, axis=2)
    pair_cross = intersection(fragment, conformer)
    pair_self = intersection(conformer, conformer)
    pair_prior = back_prior.reshape(-1)[target]
    own_atoms = to_atoms(query_atoms)
    query_self = jnp.repeat(intersection(own_atoms, own_atoms), listed)
    shape = pair_cross / (query_self + pair_self - pair_cross)
    live = jnp.arange(listed, dtype=jnp.int32)[None, :] < candidate_count[:, None]
    rescore = jnp.where(live, (shape + pair_prior).reshape(local_queries, listed), 0.0)
    return (tversky, rescore)


def solution(mesh):
    return jax.shard_map(
        body,
        mesh=mesh,
        in_specs=(
            P("qry", None),
            P(("lib", "qry"), None),
            P(("qry", "lib"), None),
            P(("lib", "qry"), None),
            P(("qry", "lib"), None),
            P(("qry", "lib")),
            P(),
        ),
        out_specs=(P(None, ("lib", "qry")), P(("qry", "lib"), None)),
        check_vma=False,
    )
```

profile of v0, /device:TPU:0, one launch (start us, length us, event | category | flops | bytes accessed | tf_op | source)
XLA Modules:
  0.0 148.4 jit_solution(1439643963473406378)
XLA Ops:
  7.2 0.9 reshape.300
  8.1 0.8 reshape.301
  8.9 3.6 %gather_fusion = s32[512]{0:T(512)S(1)} fusion(s32[24576]{0:T(1024)} %param.13, s32[1024]{0:T(1024)S(1)} %pad_clamp_fusion.1), kind=kCustom, calls=%fused_computation | custom fusion | bytes 6144 | tf_op jit(solution)/shard_map/jit(_take)/gather | solution.py:76
  12.8 2.5 %scatter_custom_fusion = s32[1152]{0:T(1024)S(1)} fusion(s32[512]{0:T(512)S(1)} %bitcast.37, s32[512]{0:T(512)S(1)} %get-tuple-element.4, s32[]{:T(128)} %constant.31.clone.1), kind=kCustom, calls=%fused_computation.44 | custom fusion | bytes 4612 | tf_op jit(solution)/shard_map/scatter | solution.py:88
  15.4 0.7 reshape.354
  16.1 6.3 %all-to-all-start = ((s32[8,1,144]{2,1,0:T(1,128)}), s32[8,1,144]{2,1,0:T(1,128)S(1)}, u32[]{:S(2)}, u32[]{:S(2)}) async-start(s32[8,1,144]{2,1,0:T(1,128)} %reshape.354), calls=%async_computation | async-start | bytes 16384 | tf_op jit(solution)/shard_map/all_to_all | solution.py:95
  22.4 0.7 all-gather.2.cloned.1.call-update
  23.1 4.9 %all-to-all-done = s32[8,1,144]{2,1,0:T(1,128)S(1)} async-done(((s32[8,1,144]{2,1,0:T(1,128)}), s32[8,1,144]{2,1,0:T(1,128)S(1)}, u32[]{:S(2)}, u32[]{:S(2)}) %all-to-all-start) | async-done | bytes 4640 | tf_op jit(solution)/shard_map/all_to_all | solution.py:95
  28.5 0.7 reduce.2
  29.3 0.7 reshape.356
  29.9 3.7 %all-to-all-start.1 = ((s32[4,1,288]{2,1,0:T(1,128)}), s32[4,1,288]{2,1,0:T(1,128)S(1)}, u32[]{:S(2)}, u32[]{:S(2)}) async-start(s32[4,1,288]{2,1,0:T(1,128)} %reshape.356), calls=%async_computation.1 | async-start | bytes 12288 | tf_op jit(solution)/shard_map/all_to_all | solution.py:94
  33.7 2.4 %scatter_custom_fusion.1 = s32[1152]{0:T(1024)S(1)} fusion(s32[512]{0:T(512)S(1)} %bitcast.38, s32[512]{0:T(512)S(1)} %fusion.19, s32[]{:T(128)} %constant.31.clone.1), kind=kCustom, calls=%fused_computation.42 | custom fusion | bytes 4612 | tf_op jit(solution)/shard_map/scatter | solution.py:91
  36.2 0.7 reshape.358
  36.9 1.4 all-to-all-done.1
  38.3 3.3 %all-to-all-start.4 = ((s32[8,1,144]{2,1,0:T(1,128)}), s32[8,1,144]{2,1,0:T(1,128)S(1)}, u32[]{:S(2)}, u32[]{:S(2)}) async-start(s32[8,1,144]{2,1,0:T(1,128)} %reshape.358), calls=%async_computation.4 | async-start | bytes 16384 | tf_op jit(solution)/shard_map/all_to_all | solution.py:102
  41.7 0.7 reduce.3
  42.6 3.4 %fusion.1 = bf16[1152,192]{0,1:T(8,128)(2,1)} fusion(f32[768,192]{0,1:T(8,128)} %param.10, s32[1152]{0:T(1024)S(1)} %eq.45), kind=kOutput, calls=%fused_computation.9 | convolution fusion | flops 2039537664 | bytes 1036800 | tf_op jit(solution)/shard_map/dot_general | solution.py:36
  46.0 2.1 %copy.98 = bf16[1152,192]{1,0:T(8,128)(2,1)} copy(bf16[1152,192]{0,1:T(8,128)(2,1)} %fusion.1) | data formatting | bytes 884736 | tf_op jit(solution)/shard_map/convert_element_type | solution.py:117
  48.0 2.1 %convert_element_type.26 = bf16[4,8,36,192]{3,2,1,0:T(8,128)(2,1)} reshape(bf16[1152,192]{1,0:T(8,128)(2,1)} %copy.98) | data formatting | bytes 884736 | tf_op jit(solution)/shard_map/convert_element_type | solution.py:117
  50.2 2.4 %copy.99 = bf16[4,8,36,192]{3,0,2,1:T(4,128)(2,1)} copy(bf16[4,8,36,192]{3,2,1,0:T(8,128)(2,1)} %convert_element_type.26) | data formatting | bytes 884736 | tf_op jit(solution)/shard_map/convert_element_type | solution.py:117
  52.5 5.0 %all-to-all-start.2 = ((bf16[4,8,36,192]{3,0,2,1:T(4,128)(2,1)}), bf16[4,8,36,192]{3,0,2,1:T(4,128)(2,1)}, u32[]{:S(2)}, u32[]{:S(2)}) async-start(bf16[4,8,36,192]{3,0,2,1:T(4,128)(2,1)} %copy.99), calls=%async_computation.2 | async-start | bytes 1179648 | tf_op jit(solution)/shard_map/all_to_all | solution.py:116
  58.0 0.9 multiply_reduce_fusion.3
  58.9 0.7 reduce.4
  59.7 0.7 reshape.360
  60.4 14.1 %all-to-all-done.2 = bf16[4,8,36,192]{3,0,2,1:T(4,128)(2,1)} async-done(((bf16[4,8,36,192]{3,0,2,1:T(4,128)(2,1)}), bf16[4,8,36,192]{3,0,2,1:T(4,128)(2,1)}, u32[]{:S(2)}, u32[]{:S(2)}) %all-to-all-start.2) | async-done | bytes 442400 | tf_op jit(solution)/shard_map/all_to_all | solution.py:116
  74.4 3.2 %all-to-all-start.5 = ((s32[4,1,288]{2,1,0:T(1,128)}), s32[4,1,288]{2,1,0:T(1,128)S(1)}, u32[]{:S(2)}, u32[]{:S(2)}) async-start(s32[4,1,288]{2,1,0:T(1,128)} %reshape.360), calls=%async_computation.5 | async-start | bytes 12288 | tf_op jit(solution)/shard_map/all_to_all | solution.py:101
  78.4 0.7 broadcast_in_dim.48
  79.2 0.7 broadcast_in_dim.52
  80.1 0.7 broadcast_in_dim.54
  81.0 0.7 broadcast_in_dim.56
  81.7 2.1 %copy.100 = bf16[4,8,36,192]{3,1,2,0:T(8,128)(2,1)} copy(bf16[4,8,36,192]{3,0,2,1:T(4,128)(2,1)} %all-to-all-done.2) | data formatting | bytes 884736 | tf_op jit(solution)/shard_map/all_to_all | solution.py:116
  83.8 4.2 %all-to-all-start.3 = ((bf16[4,8,36,192]{3,1,2,0:T(8,128)(2,1)}), bf16[4,8,36,192]{3,1,2,0:T(8,128)(2,1)}, u32[]{:S(2)}, u32[]{:S(2)}) async-start(bf16[4,8,36,192]{3,1,2,0:T(8,128)(2,1)} %copy.100), calls=%async_computation.3 | async-start | bytes 1179648 | tf_op jit(solution)/shard_map/all_to_all | solution.py:115
  88.1 0.7 reduce.5
  89.0 7.8 %all-to-all-done.3 = bf16[4,8,36,192]{3,1,2,0:T(8,128)(2,1)} async-done(((bf16[4,8,36,192]{3,1,2,0:T(8,128)(2,1)}), bf16[4,8,36,192]{3,1,2,0:T(8,128)(2,1)}, u32[]{:S(2)}, u32[]{:S(2)}) %all-to-all-start.3) | async-done | bytes 442400 | tf_op jit(solution)/shard_map/all_to_all | solution.py:115
  96.8 2.0 %copy.101 = bf16[4,8,36,192]{3,2,1,0:T(8,128)(2,1)} copy(bf16[4,8,36,192]{3,1,2,0:T(8,128)(2,1)} %all-to-all-done.3) | data formatting | bytes 884736 | tf_op jit(solution)/shard_map/all_to_all | solution.py:115
  98.8 2.1 %reshape.303 = bf16[1152,192]{1,0:T(8,128)(2,1)} reshape(bf16[4,8,36,192]{3,2,1,0:T(8,128)(2,1)} %copy.101) | data formatting | bytes 884736 | tf_op jit(solution)/shard_map/reshape | solution.py:134
  101.0 2.4 %fusion.2 = f32[192,512]{1,0:T(8,128)} fusion(bf16[1152,192]{1,0:T(8,128)(2,1)} %reshape.303, s32[512]{0:T(512)S(1)} %multiply_add_fusion), kind=kOutput, calls=%fused_computation.11 | convolution fusion | flops 227082240 | bytes 837632 | tf_op jit(solution)/shard_map/dot_general | solution.py:24
  103.4 1.5 %multiply_reduce_fusion.2 = f32[256]{0:T(256)S(1)} fusion(bf16[256,2048]{1,0:T(8,128)(2,1)} %all-gather.2.cloned.1.call-done), kind=kLoop, calls=%fused_computation.12 | loop fusion | flops 1572608 | bytes 1049600 | tf_op jit(solution)/shard_map/reduce_sum | solution.py:14
  104.9 2.2 %fusion.4 = bf16[256,768]{1,0:T(8,128)(2,1)S(1)} fusion(bf16[256,2048]{1,0:T(8,128)(2,1)} %all-gather.2.cloned.1.call-done, bf16[768,2048]{1,0:T(8,128)(2,1)S(1)} %copy-done, f32[256]{0:T(256)S(1)} %broadcast_add_fusion), kind=kOutput, calls=%fused_computation.15 | convolution fusion | flops 805699584 | bytes 4588544 | tf_op jit(solution)/shard_map/dot_general | solution.py:11
  107.2 9.9 %gather_fusion.1 = bf16[1152]{0:T(1024)(128)(2,1)S(1)} fusion(bf16[256,768]{1,0:T(8,128)(2,1)S(1)} %fusion.4, s32[1152]{0:T(1024)S(1)} %fusion.12), kind=kCustom, calls=%fused_computation.1 | custom fusion | bytes 13824 | tf_op jit(solution)/shard_map/gather | solution.py:113
  117.8 3.3 %all-to-all-start.6 = ((bf16[4,8,36]{2,0,1:T(4,128)(2,1)}), bf16[4,8,36]{2,0,1:T(4,128)(2,1)S(1)}, u32[]{:S(2)}, u32[]{:S(2)}) async-start(bf16[4,8,36]{2,0,1:T(4,128)(2,1)} %copy.111), calls=%async_computation.6 | async-start | bytes 16384 | tf_op jit(solution)/shard_map/all_to_all | solution.py:125
  121.2 1.8 %fusion.24 = (f32[48,512]{1,0:T(8,128)}, f32[48,512]{1,0:T(8,128)}, f32[48,512]{1,0:T(8,128)}, f32[48,512]{1,0:T(8,128)}) fusion(f32[192,512]{1,0:T(8,128)} %fusion.2), kind=kLoop, calls=%fused_computation.60 | loop fusion | bytes 786432 | tf_op jit(solution)/shard_map/slice | solution.py:54
  122.9 3.8 %all-to-all-done.6 = bf16[4,8,36]{2,0,1:T(4,128)(2,1)S(1)} async-done(((bf16[4,8,36]{2,0,1:T(4,128)(2,1)}), bf16[4,8,36]{2,0,1:T(4,128)(2,1)S(1)}, u32[]{:S(2)}, u32[]{:S(2)}) %all-to-all-start.6) | async-done | bytes 2336 | tf_op jit(solution)/shard_map/all_to_all | solution.py:125
  126.7 0.7 reshape.362
  127.4 3.2 %all-to-all-start.7 = ((bf16[4,2,144]{2,1,0:T(2,128)(2,1)}), bf16[4,2,144]{2,1,0:T(2,128)(2,1)S(1)}, u32[]{:S(2)}, u32[]{:S(2)}) async-start(bf16[4,2,144]{2,1,0:T(2,128)(2,1)} %reshape.362), calls=%async_computation.7 | async-start | bytes 8192 | tf_op jit(solution)/shard_map/all_to_all | solution.py:124
  130.6 5.8 %multiply_reduce_fusion = (f32[512]{0:T(512)S(1)}, f32[512]{0:T(512)S(1)}) fusion(f32[48,512]{1,0:T(8,128)} %get-tuple-element.7, f32[48,512]{1,0:T(8,128)} %get-tuple-element.8, f32[48,512]{1,0:T(8,128)} %get-tuple-element.9, f32[48,512]{1,0:T(8,128)} %get-tuple-element.6, f32[48,512]{1,0:T(8,128)} %broadcast_in_dim.56, f32[48,512]{1,0:T(8,128)} %broadcast_in_dim.54, ...), kind=kLoop, calls=%fused_computation.5 | loop fusion | flops 28310528 | bytes 790528 | tf_op jit(solution)/shard_map/reduce_sum | solution.py:53
  136.9 3.3 %gather_fusion.2 = f32[512]{0:T(512)S(1)} fusion(f32[1152]{0:T(1024)S(1)} %reshape.310, s32[1024]{0:T(1024)} %pad_clamp_fusion), kind=kCustom, calls=%fused_computation.2 | custom fusion | bytes 6144 | tf_op jit(solution)/shard_map/gather | solution.py:138
  140.2 1.3 fusion.14
  (55 shorter events, 4.4 us)
Async XLA Ops:
  7.2 97.8 %copy-start = (bf16[768,2048]{1,0:T(8,128)(2,1)S(1)}, bf16[768,2048]{1,0:T(8,128)(2,1)}, u32[]{:S(2)}) copy-start(bf16[768,2048]{1,0:T(8,128)(2,1)} %param.8) | copy-start | bytes 9437188
  16.1 11.9 %all-to-all-start = ((s32[8,1,144]{2,1,0:T(1,128)}), s32[8,1,144]{2,1,0:T(1,128)S(1)}, u32[]{:S(2)}, u32[]{:S(2)}) async-start(s32[8,1,144]{2,1,0:T(1,128)} %reshape.354), calls=%async_computation | async-start | bytes 16384 | tf_op jit(solution)/shard_map/all_to_all | solution.py:95
  22.4 81.0 %all-gather.2.cloned.1.call-start = ((), (), s32[]{:S(2)}) async-start(), calls=%async_computation.8 | async-start | bytes 1179648 | tf_op jit(solution)/shard_map/all_gather | solution.py:75
  29.9 8.4 %all-to-all-start.1 = ((s32[4,1,288]{2,1,0:T(1,128)}), s32[4,1,288]{2,1,0:T(1,128)S(1)}, u32[]{:S(2)}, u32[]{:S(2)}) async-start(s32[4,1,288]{2,1,0:T(1,128)} %reshape.356), calls=%async_computation.1 | async-start | bytes 12288 | tf_op jit(solution)/shard_map/all_to_all | solution.py:94
  38.3 14.2 %all-to-all-start.4 = ((s32[8,1,144]{2,1,0:T(1,128)}), s32[8,1,144]{2,1,0:T(1,128)S(1)}, u32[]{:S(2)}, u32[]{:S(2)}) async-start(s32[8,1,144]{2,1,0:T(1,128)} %reshape.358), calls=%async_computation.4 | async-start | bytes 16384 | tf_op jit(solution)/shard_map/all_to_all | solution.py:102
  42.6 15.0 %copy-start.2 = (f32[8,192]{1,0:T(8,128)S(1)}, f32[8,192]{1,0:T(8,128)}, u32[]{:S(2)}) copy-start(f32[8,192]{1,0:T(8,128)} %param.9) | copy-start | bytes 18436
  52.5 21.9 %all-to-all-start.2 = ((bf16[4,8,36,192]{3,0,2,1:T(4,128)(2,1)}), bf16[4,8,36,192]{3,0,2,1:T(4,128)(2,1)}, u32[]{:S(2)}, u32[]{:S(2)}) async-start(bf16[4,8,36,192]{3,0,2,1:T(4,128)(2,1)} %copy.99), calls=%async_computation.2 | async-start | bytes 1179648 | tf_op jit(solution)/shard_map/all_to_all | solution.py:116
  74.4 9.3 %all-to-all-start.5 = ((s32[4,1,288]{2,1,0:T(1,128)}), s32[4,1,288]{2,1,0:T(1,128)S(1)}, u32[]{:S(2)}, u32[]{:S(2)}) async-start(s32[4,1,288]{2,1,0:T(1,128)} %reshape.360), calls=%async_computation.5 | async-start | bytes 12288 | tf_op jit(solution)/shard_map/all_to_all | solution.py:101
  83.8 13.0 %all-to-all-start.3 = ((bf16[4,8,36,192]{3,1,2,0:T(8,128)(2,1)}), bf16[4,8,36,192]{3,1,2,0:T(8,128)(2,1)}, u32[]{:S(2)}, u32[]{:S(2)}) async-start(bf16[4,8,36,192]{3,1,2,0:T(8,128)(2,1)} %copy.100), calls=%async_computation.3 | async-start | bytes 1179648 | tf_op jit(solution)/shard_map/all_to_all | solution.py:115
  107.2 29.3 %copy-start.1 = (bf16[256,768]{1,0:T(8,128)(2,1)}, bf16[256,768]{1,0:T(8,128)(2,1)S(1)}, u32[]{:S(2)}) copy-start(bf16[256,768]{1,0:T(8,128)(2,1)S(1)} %fusion.4) | copy-start | bytes 1179652
  117.8 8.9 %all-to-all-start.6 = ((bf16[4,8,36]{2,0,1:T(4,128)(2,1)}), bf16[4,8,36]{2,0,1:T(4,128)(2,1)S(1)}, u32[]{:S(2)}, u32[]{:S(2)}) async-start(bf16[4,8,36]{2,0,1:T(4,128)(2,1)} %copy.111), calls=%async_computation.6 | async-start | bytes 16384 | tf_op jit(solution)/shard_map/all_to_all | solution.py:125
  127.4 9.3 %all-to-all-start.7 = ((bf16[4,2,144]{2,1,0:T(2,128)(2,1)}), bf16[4,2,144]{2,1,0:T(2,128)(2,1)S(1)}, u32[]{:S(2)}, u32[]{:S(2)}) async-start(bf16[4,2,144]{2,1,0:T(2,128)(2,1)} %reshape.362), calls=%async_computation.7 | async-start | bytes 8192 | tf_op jit(solution)/shard_map/all_to_all | solution.py:124
  130.6 9.6 %copy-start.3 = (f32[8]{0:T(128)S(1)}, f32[8]{0:T(128)}, u32[]{:S(2)}) copy-start(f32[8]{0:T(128)} %multiply_reduce_fusion.3) | copy-start | bytes 100
Sparse Core Ops, SparseCore 0:
  24.8 23.5 all-gather.1
where the time goes:
time: 150 us; the launch traced here: 148 us
  local copies, waits for them, and re-layouts  47.7 us (32%)
  waiting for transfers between devices  32.6 us (22%)
  starting transfers between devices  32.4 us (22%)
  between operations  14.3 us (10%)
  other arithmetic  13.2 us (9%)
  matrix products  8.09 us (5%)
    all_to_all x1, waiting for transfers between devices, body(): lax.all_to_all(fetched.astype(jnp.bfloat16), 'qry', split_axis=1, concat_...  14.1 us
    gather x3, local copies, waits for them, and re-layouts, body(): tversky[got_query.reshape(-1), flat_slots].astype(jnp.float32)  10.6 us
    all_to_all x1, waiting for transfers between devices, body(): lax.all_to_all(lax.all_to_all(fetched.astype(jnp.bfloat16), 'qry', split_...  7.83 us
    reduce_sum x2, other arithmetic, intersection(): jnp.sum(first[3][:, None, :] * second[3][None, :, :] * jnp.exp(-SHARPNESS...  6.76 us
    convert_element_type x3, local copies, waits for them, and re-layouts, body(): fetched.astype(jnp.bfloat16)  6.56 us
    all_to_all x1, starting transfers between devices, body(): lax.all_to_all(send_slot, 'qry', split_axis=1, concat_axis=1, tiled=True)  6.33 us
    all_to_all x1, starting transfers between devices, body(): lax.all_to_all(fetched.astype(jnp.bfloat16), 'qry', split_axis=1, concat_...  5.03 us
    all_to_all x1, waiting for transfers between devices, body(): lax.all_to_all(send_slot, 'qry', split_axis=1, concat_axis=1, tiled=True)  4.87 us
  transfers between devices with their start and end apart: 9, of which 5 were waited for; matrix products, arithmetic and copies ran while one was open for 27% of the time, Pallas kernels for 0%

commit v1 on v0

v1 whole, which is shorter than its diff:
```python
import functools
import math

import jax
import jax.numpy as jnp
from jax import lax
from jax.experimental import pallas as pl
from jax.experimental.pallas import tpu as pltpu
from jax.sharding import PartitionSpec as P

SHARPNESS = 0.8
EPSILON = 1e-06
LANES = 128
CORES = 2
SCALE = SHARPNESS * math.log2(math.e)
ROOT = math.sqrt(2.0 * SCALE)

F32 = jnp.float32
BF16 = jnp.bfloat16
I32 = jnp.int32


def nt(a, b):
    return lax.dot_general(a, b, (((1,), (1,)), ((), ())), preferred_element_type=F32)


def nn(a, b):
    return lax.dot_general(a, b, (((1,), (0,)), ((), ())), preferred_element_type=F32)


def split2(x):
    hi = x.astype(BF16)
    return hi, (x - hi.astype(F32)).astype(BF16)


def iota(shape, dim):
    return lax.broadcasted_iota(I32, shape, dim)


def fdiv(x, by):
    return jnp.floor((x.astype(F32) + 0.5) * (1.0 / by)).astype(I32)


def prepare(x, y, z, w):
    norm = SCALE * (x * x + y * y + z * z)
    return x * ROOT, y * ROOT, z * ROOT, w * jnp.exp2(-norm)


def self_overlap(ref, lanes, atoms):
    blocks = atoms // 8
    comp = [[ref[pl.ds(c * atoms + 8 * i, 8), lanes] for i in range(blocks)] for c in range(4)]
    total = None
    diag = [None] * blocks
    off = [None] * blocks
    for a in range(atoms):
        xa, ya, za, wa = (ref[pl.ds(c * atoms + a, 1), lanes] for c in range(4))
        wa2 = wa + wa
        for i in range(a // 8, blocks):
            e = jnp.exp2(xa * comp[0][i] + ya * comp[1][i] + za * comp[2][i])
            if i == a // 8:
                diag[i] = wa * e if diag[i] is None else diag[i] + wa * e
            else:
                off[i] = wa2 * e if off[i] is None else off[i] + wa2 * e
    for i in range(blocks):
        part = diag[i] if off[i] is None else diag[i] + off[i]
        part = part * comp[3][i]
        total = part if total is None else total + part
    return jnp.sum(total, axis=0, keepdims=True)


def cross_overlap(qref, cref, lanes, atoms):
    comp = [cref[pl.ds(c * atoms, atoms), lanes] for c in range(4)]
    acc = None
    for a in range(atoms):
        xa, ya, za, wa = (qref[pl.ds(c * atoms + a, 1), lanes] for c in range(4))
        e = wa * jnp.exp2(xa * comp[0] + ya * comp[1] + za * comp[2])
        acc = e if acc is None else acc + e
    return jnp.sum(acc * comp[3], axis=0, keepdims=True)


def kernel(
    nq, nl, cap, id_bytes,
    qp_ref, lib_hbm, qa_ref, conf_hbm, cand_ref, count_ref, home_ref,
    tv_ref, out_ref,
    lib, conf, gath, pack, atoms_in, bucket, codes_in, ret_out, ret_in,
    confp, qprep, pairs_c, pairs_q, onehot, qonehot, cself, qself, shape_s, valid_s,
    loc_sem, s1_send, s1_recv, sib_send, sib_recv, s2_send, s2_recv,
    at_send, at_recv, co_send, co_recv, re_send, re_recv,
):
    q = lax.axis_index("qry")
    l = lax.axis_index("lib")
    dev = nq * nl
    me = q * nl + l
    nz = nq // CORES
    z, c = q // CORES, lax.rem(q, CORES)
    sib = z * CORES + (1 - c)
    own_rows = lib.shape[0]
    block = qp_ref.shape[0]
    cols = gath.shape[2]
    local_q, listed = cand_ref.shape
    cand_n = local_q * listed
    atoms = qa_ref.shape[1] // 4
    half = 2 * atoms
    pairs = onehot.shape[1]

    def target(d):
        t = lax.rem(me + d, dev)
        return t, {"qry": t // nl, "lib": lax.rem(t, nl)}

    barrier = pltpu.get_barrier_semaphore()

    def greet(d, carry):
        _, where = target(d)
        pl.semaphore_signal(barrier, inc=1, device_id=where, device_id_type=pl.DeviceIdType.MESH)
        return carry

    lax.fori_loop(1, dev, greet, 0)

    lib_copy = pltpu.make_async_copy(lib_hbm, lib, loc_sem.at[0])
    conf_copy = pltpu.make_async_copy(conf_hbm, conf, loc_sem.at[1])
    conf_copy.start()
    lib_copy.start()

    qa = qa_ref[...]
    zero = jnp.zeros((local_q, LANES - half), F32)
    top = jnp.concatenate([qa[:, :half], zero], axis=1)
    low = jnp.concatenate([qa[:, half:], zero], axis=1)
    pack[...] = jnp.concatenate([top, low], axis=0).astype(BF16)

    ids = jnp.concatenate([cand_ref[pl.ds(i, 1), :] for i in range(local_q)], axis=1)
    table = home_ref[...]
    trows = table.shape[0]
    pieces = [
        jnp.transpose(((table >> (8 * k)) & 255).astype(F32)).astype(BF16) for k in range(id_bytes)
    ]
    row_hot = jnp.where(iota((trows, cand_n), 0) == (ids >> 7), 1.0, 0.0).astype(BF16)
    lane_hot = iota((LANES, cand_n), 0) == (ids & 127)
    stored = jnp.zeros((1, cand_n), I32)
    for k in range(id_bytes):
        found = nn(pieces[k], row_hot)
        byte = jnp.sum(jnp.where(lane_hot, found, 0.0), axis=0, keepdims=True)
        stored = stored + (byte.astype(I32) << (8 * k))
    owner = fdiv(stored, own_rows)
    slot = stored - owner * own_rows
    owner_l = fdiv(owner, nq)
    owner_s = (owner - owner_l * nq) * nl + owner_l

    owns = iota((dev, cand_n), 0) == owner_s
    owns_b = jnp.where(owns, 1.0, 0.0).astype(BF16)
    tri = jnp.where(iota((cand_n, cand_n), 0) < iota((cand_n, cand_n), 1), 1.0, 0.0).astype(BF16)
    before = nn(owns_b, tri)
    rank = jnp.sum(jnp.where(owns, before, 0.0), axis=0, keepdims=True).astype(I32)
    rank_hot = iota((LANES, cand_n), 0) == rank
    rank_b = jnp.where(rank_hot, 1.0, 0.0).astype(BF16)
    code = slot * local_q + fdiv(iota((1, cand_n), 1), listed) + 1
    lo = (code & 127).astype(F32)
    hi = (code >> 7).astype(F32)
    left = jnp.concatenate([jnp.where(owns, lo, 0.0), jnp.where(owns, hi, 0.0)], axis=0).astype(BF16)
    sums = nt(left, rank_b).astype(I32)
    codes = sums[:dev] + (sums[dev:] << 7)
    for o in range(dev):
        bucket[o] = codes[o : o + 1]

    pl.semaphore_wait(barrier, dev - 1)

    def remote(src, dst, ssem, rsem, dq, dl):
        return pltpu.make_async_remote_copy(
            src_ref=src, dst_ref=dst, send_sem=ssem, recv_sem=rsem,
            device_id={"qry": dq, "lib": dl}, device_id_type=pl.DeviceIdType.MESH,
        )

    def piece(bq, k):
        return gath.at[k, pl.ds(pl.multiple_of(bq * block, block), block), :]

    def stage1(d):
        return remote(
            qp_ref.at[:, pl.ds(pl.multiple_of(l * cols, cols), cols)], piece(q, l),
            s1_send.at[d], s1_recv.at[d], lax.rem(z + d, nz) * CORES + c, l,
        )

    def from_z(d):
        return lax.rem(z - d + nz, nz) * CORES + c

    def stage2(d, e):
        there = piece(from_z(d), l)
        return remote(there, there, s2_send.at[d, e], s2_recv.at[d, e], q, lax.rem(l + e, nl))

    def to_sib(bq, k, i, j):
        there = piece(bq, k)
        return remote(there, there, sib_send.at[i, j], sib_recv.at[i, j], sib, l)

    def from_l(e):
        return lax.rem(l - e + nl, nl)

    def sib_block(d):
        return lax.rem(z - d + nz, nz) * CORES + (1 - c)

    for d in range(1, nz):
        stage1(d).start()
    for k in range(nl):
        gath[k, pl.ds(pl.multiple_of(q * block, block), block), :] = qp_ref[:, k * cols : (k + 1) * cols]
    for k in range(nl):
        to_sib(q, k, 0, k).start()

    def pairwise(src, dst, ssem, rsem):
        def make(d):
            t, where = target(d)
            return pltpu.make_async_remote_copy(
                src_ref=src(t), dst_ref=dst, send_sem=ssem.at[d], recv_sem=rsem.at[d],
                device_id=where, device_id_type=pl.DeviceIdType.MESH,
            )
        return make

    send_code = pairwise(lambda t: bucket.at[t], codes_in.at[me], co_send, co_recv)
    send_atom = pairwise(lambda t: pack, atoms_in.at[me], at_send, at_recv)
    send_back = pairwise(lambda t: ret_out.at[t], ret_in.at[me], re_send, re_recv)

    def launch(d, carry):
        send_code(d).start()
        send_atom(d).start()
        return carry

    lax.fori_loop(1, dev, launch, 0)
    codes_in[me] = bucket[me]
    atoms_in[me] = pack[...]

    conf_copy.wait()
    conf_t = jnp.transpose(conf[...])
    comps = prepare(*(conf_t[i * atoms : (i + 1) * atoms] for i in range(4)))
    for i in range(4):
        confp[i * atoms : (i + 1) * atoms] = comps[i]

    def self_step(g, carry):
        lanes = pl.ds(pl.multiple_of(g * LANES, LANES), LANES)
        cself[0:1, lanes] = self_overlap(confp, lanes, atoms)
        return carry

    lax.fori_loop(0, own_rows // LANES, self_step, 0)

    for d in range(1, nz):
        stage1(d).wait_recv()
        for e in range(1, nl):
            stage2(d, e).start()
        to_sib(from_z(d), l, d, 0).start()

    def landed(d, carry):
        send_code(d).wait_recv()
        send_atom(d).wait_recv()
        return carry

    lax.fori_loop(1, dev, landed, 0)

    got = codes_in[...].reshape(dev, LANES)
    pair_at = iota((1, pairs), 1)
    pair_src = fdiv(pair_at, cap)
    pair_j = pair_at - pair_src * cap
    j_hot = jnp.where(iota((LANES, pairs), 0) == pair_j, 1.0, 0.0).astype(BF16)
    src_hot = iota((dev, pairs), 0) == pair_src
    both = jnp.concatenate([got & 127, got >> 7], axis=0).astype(F32).astype(BF16)
    spread = nn(both, j_hot)
    low7 = jnp.sum(jnp.where(src_hot, spread[:dev], 0.0), axis=0, keepdims=True).astype(I32)
    high = jnp.sum(jnp.where(src_hot, spread[dev:], 0.0), axis=0, keepdims=True).astype(I32)
    pcode = low7 + (high << 7)
    valid_s[...] = jnp.where(pcode > 0, 1.0, 0.0)
    pcode = jnp.maximum(pcode - 1, 0)
    pslot = fdiv(pcode, local_q)
    pquery = pair_src * local_q + (pcode - pslot * local_q)
    onehot[...] = jnp.where(iota((own_rows, pairs), 0) == pslot, 1.0, 0.0).astype(BF16)
    qonehot[...] = jnp.where(iota((dev * local_q, pairs), 0) == pquery, 1.0, 0.0).astype(BF16)

    raw = atoms_in[...].astype(F32)
    q_top = jnp.transpose(raw[:, :local_q].reshape(dev * local_q, LANES))
    q_low = jnp.transpose(raw[:, local_q:].reshape(dev * local_q, LANES))
    comps = prepare(q_top[:atoms], q_top[atoms:half], q_low[:atoms], q_low[atoms:half])
    for i in range(4):
        qprep[i * atoms : (i + 1) * atoms] = comps[i]

    def qself_step(g, carry):
        lanes = pl.ds(pl.multiple_of(g * LANES, LANES), LANES)
        qself[0:1, lanes] = self_overlap(qprep, lanes, atoms)
        return carry

    lax.fori_loop(0, dev * local_q // LANES, qself_step, 0)

    pad = jnp.zeros((7, own_rows), F32)
    hi_c, lo_c = split2(jnp.concatenate([confp[...], cself[...], pad], axis=0))
    pairs_c[...] = nn(hi_c, onehot[...]) + nn(lo_c, onehot[...])
    pad = jnp.zeros((7, dev * local_q), F32)
    hi_q, lo_q = split2(jnp.concatenate([qprep[...], qself[...], pad], axis=0))
    pairs_q[...] = nn(hi_q, qonehot[...]) + nn(lo_q, qonehot[...])

    def cross_step(g, carry):
        lanes = pl.ds(pl.multiple_of(g * LANES, LANES), LANES)
        cross = cross_overlap(pairs_q, pairs_c, lanes, atoms)
        selves = pairs_q[4 * atoms : 4 * atoms + 1, lanes] + pairs_c[4 * atoms : 4 * atoms + 1, lanes]
        shape_s[0:1, lanes] = cross / (selves - cross)
        return carry

    groups = pairs // LANES
    first = groups // 3
    lax.fori_loop(0, first, cross_step, 0)

    for d in range(1, nz):
        for e in range(1, nl):
            stage2(d, e).wait_recv()
            to_sib(from_z(d), from_l(e), d, e).start()

    lax.fori_loop(first, groups, cross_step, 0)

    def sib_wait(bq, k, i, j):
        to_sib(bq, k, i, j).wait_recv()

    for k in range(nl):
        sib_wait(sib, k, 0, k)
    for d in range(1, nz):
        sib_wait(sib_block(d), l, d, 0)
        for e in range(1, nl):
            sib_wait(sib_block(d), from_l(e), d, e)
    lib_copy.wait()

    rows = nq * block
    chunk = min(rows, 256)
    priors = None
    for r in range(0, rows, chunk):
        scores = None
        norms = None
        for k in range(nl):
            part = gath[k, r : r + chunk, :]
            prod = nt(part, lib[:, k * cols : (k + 1) * cols])
            wide = part.astype(F32)
            sq = jnp.sum(wide * wide, axis=1, keepdims=True)
            scores = prod if scores is None else scores + prod
            norms = sq if norms is None else norms + sq
        tv = (scores / (norms + EPSILON)).astype(BF16)
        tv_ref[r : r + chunk, :] = tv
        chosen = nn(tv, onehot[...]) * qonehot[r : r + chunk, :].astype(F32)
        chosen = jnp.sum(chosen, axis=0, keepdims=True)
        priors = chosen if priors is None else priors + chosen

    score = jnp.where(valid_s[...] > 0.0, shape_s[...] + priors, 0.0)
    hi_s, lo_s = split2(jnp.where(src_hot, score, 0.0))
    back = nt(hi_s, j_hot) + nt(lo_s, j_hot)
    for s in range(dev):
        ret_out[s] = back[s : s + 1]

    def launch_back(d, carry):
        send_back(d).start()
        return carry

    lax.fori_loop(1, dev, launch_back, 0)
    ret_in[me] = ret_out[me]

    for d in range(1, nz):
        stage1(d).wait_send()
        to_sib(from_z(d), l, d, 0).wait_send()
        for e in range(1, nl):
            stage2(d, e).wait_send()
            to_sib(from_z(d), from_l(e), d, e).wait_send()
    for k in range(nl):
        to_sib(q, k, 0, k).wait_send()

    def settle(d, carry):
        send_code(d).wait_send()
        send_atom(d).wait_send()
        return carry

    lax.fori_loop(1, dev, settle, 0)

    def landed_back(d, carry):
        send_back(d).wait_recv()
        return carry

    lax.fori_loop(1, dev, landed_back, 0)

    came = jnp.transpose(ret_in[...].reshape(dev, LANES))
    hi_b, lo_b = split2(came)
    mine = nn(hi_b, owns_b) + nn(lo_b, owns_b)
    final = jnp.sum(jnp.where(rank_hot, mine, 0.0), axis=0, keepdims=True)
    for i in range(local_q):
        line = final[:, i * listed : (i + 1) * listed]
        live = iota((1, listed), 1) < count_ref[i]
        out_ref[i : i + 1, :] = jnp.where(live, line, 0.0)

    def settle_back(d, carry):
        send_back(d).wait_send()
        return carry

    lax.fori_loop(1, dev, settle_back, 0)


def body(nq, nl, query_prints, library_prints, query_atoms, conformer_atoms, candidates, candidate_count, home_row):
    dev = nq * nl
    block, width = query_prints.shape
    own_rows = library_prints.shape[0]
    local_q, listed = candidates.shape
    atoms = query_atoms.shape[1] // 4
    cand_n = local_q * listed
    cap = 2 * ((cand_n + dev - 1) // dev) + 4
    pairs = (dev * cap + LANES - 1) // LANES * LANES
    id_bytes = ((home_row.shape[0] - 1).bit_length() + 7) // 8
    rows = nq * block
    nz = nq // CORES
    vm = pltpu.VMEM
    dma = pltpu.SemaphoreType.DMA
    vspec = pl.BlockSpec(memory_space=pltpu.VMEM)
    aspec = pl.BlockSpec(memory_space=pl.ANY)
    return pl.pallas_call(
        functools.partial(kernel, nq, nl, cap, id_bytes),
        out_shape=(
            jax.ShapeDtypeStruct((rows, own_rows), BF16),
            jax.ShapeDtypeStruct((local_q, listed), F32),
        ),
        in_specs=[
            vspec, aspec, vspec, aspec, vspec, pl.BlockSpec(memory_space=pltpu.SMEM), vspec,
        ],
        out_specs=(vspec, vspec),
        scratch_shapes=[
            vm((own_rows, width), BF16),
            vm((own_rows, 4 * atoms), F32),
            vm((nl, rows, width // nl), BF16),
            vm((2 * local_q, LANES), BF16),
            vm((dev, 2 * local_q, LANES), BF16),
            vm((dev, 1, LANES), I32),
            vm((dev, 1, LANES), I32),
            vm((dev, 1, LANES), F32),
            vm((dev, 1, LANES), F32),
            vm((4 * atoms, own_rows), F32),
            vm((4 * atoms, rows), F32),
            vm((4 * atoms + 8, pairs), F32),
            vm((4 * atoms + 8, pairs), F32),
            vm((own_rows, pairs), BF16),
            vm((rows, pairs), BF16),
            vm((1, own_rows), F32),
            vm((1, rows), F32),
            vm((1, pairs), F32),
            vm((1, pairs), F32),
            dma((2,)),
            dma((nz,)), dma((nz,)),
            dma((nz, nl)), dma((nz, nl)),
            dma((nz, nl)), dma((nz, nl)),
            dma((dev,)), dma((dev,)),
            dma((dev,)), dma((dev,)),
            dma((dev,)), dma((dev,)),
        ],
        compiler_params=pltpu.CompilerParams(
            collective_id=0, has_side_effects=True, vmem_limit_bytes=56 * 1024 * 1024
        ),
    )(
        query_prints, library_prints, query_atoms, conformer_atoms, candidates, candidate_count,
        home_row.reshape(-1, LANES),
    )


def solution(mesh):
    return jax.shard_map(
        functools.partial(body, mesh.shape["qry"], mesh.shape["lib"]),
        mesh=mesh,
        in_specs=(
            P("qry", None),
            P(("lib", "qry"), None),
            P(("qry", "lib"), None),
            P(("lib", "qry"), None),
            P(("qry", "lib"), None),
            P(("qry", "lib")),
            P(),
        ),
        out_specs=(P(None, ("lib", "qry")), P(("qry", "lib"), None)),
        check_vma=False,
    )
```

time: 150 us -> 39.5 us (0.26)
  local copies, waits for them, and re-layouts: 47.7 us -> 5.25 us
  Pallas kernels: 0 us -> 33.4 us
  waiting for transfers between devices: 32.6 us -> 0 us
  starting transfers between devices: 32.4 us -> 0 us
  between operations: 14.3 us -> 0.64 us
  other arithmetic: 13.2 us -> 0 us
  matrix products: 8.09 us -> 0 us
    pallas_call x0 -> x1, Pallas kernels: none -> 33.4 us  [body(): pl.pallas_call(functools.partial(kernel, nq, nl, cap, id_bytes), out_shap...]
    all_to_all x8 -> x0, starting transfers between devices: 32.4 us -> none  [the longest x1 6.33 us: body(): lax.all_to_all(send_slot, 'qry', split_axis=1, concat_axis=1, tiled=True)]
    all_to_all x8 -> x0, waiting for transfers between devices: 32 us -> none  [the longest x1 14.1 us: body(): lax.all_to_all(fetched.astype(jnp.bfloat16), 'qry', split_axis=1, concat_...]
    gather x6 -> x0, local copies, waits for them, and re-layouts: 17.6 us -> none  [the longest x3 10.6 us: body(): tversky[got_query.reshape(-1), flat_slots].astype(jnp.float32)]
    reduce_sum x4 -> x0, other arithmetic: 8.53 us -> none  [the longest x2 6.76 us: intersection(): jnp.sum(first[3][:, None, :] * second[3][None, :, :] * jnp.exp(-SHARPNESS...]
    dot_general x3 -> x0, matrix products: 8.09 us -> none  [the longest x1 3.41 us: pick_rows(): lax.dot_general(picks, table, (((0,), (0,)), ((), ())), precision=lax.Pre...]
    convert_element_type x3 -> x0, local copies, waits for them, and re-layouts: 6.56 us -> none  [body(): fetched.astype(jnp.bfloat16)]
    scatter x2 -> x0, local copies, waits for them, and re-layouts: 4.9 us -> none  [the longest x1 2.45 us: body(): jnp.zeros(devices * capacity, jnp.int32).at[target].set(slot_index)]
  transfers between devices with their start and end apart: 9 -> 0, of which waited for: 5 -> 0; matrix products, arithmetic and copies ran while one was open for 27% -> 0% of each run, Pallas kernels for 0% -> 0%
where the time goes in v1:
time: 39.5 us; the launch traced here: 39.3 us
  Pallas kernels  33.4 us (85%)
  local copies, waits for them, and re-layouts  5.25 us (13%)
  between operations  0.64 us (2%)
    pallas_call x1, Pallas kernels, body(): pl.pallas_call(functools.partial(kernel, nq, nl, cap, id_bytes), out_shap...  33.4 us
    unnamed x3, local copies, waits for them, and re-layouts  5.25 us

profile of v1, /device:TPU:0, one launch (start us, length us, event | category | flops | bytes accessed | tf_op | source)
XLA Modules:
  0.0 39.3 jit_solution(13131385831100557929)
XLA Ops:
  0.6 2.2 %copy.9.conf_hbm = f32[768,192]{1,0:T(8,128)} copy(f32[768,192]{0,1:T(8,128)} %param.10) | data formatting | bytes 1179648 | tf_op args[3]
  2.8 33.4 %shard_map.86 = (bf16[256,768]{1,0:T(8,128)(2,1)}, f32[8,64]{1,0:T(8,128)}) custom-call(bf16[32,2048]{1,0:T(8,128)(2,1)} %qp_ref.1, bf16[768,2048]{1,0:T(8,128)(2,1)} %lib_hbm.1, f32[8,192]{1,0:T(8,128)} %qa_ref.1, f32[768,192]{1,0:T(8,128)} %copy.9.conf_hbm, s32[8,64]{1,0:T(8,128)} %cand_ref.1, s32[8]{0:T(128)} %count_ref.1, s32[192,128]{1,0:T(8,128)} %bitcast.1), custom_call_target="tpu_custom_call" | custom-call | tf_op jit(solution)/shard_map/pallas_call | solution.py:407
  36.3 1.8 %copy.12 = bf16[256,768]{1,0:T(8,128)(2,1)} copy(bf16[256,768]{1,0:T(8,128)(2,1)} %get-tuple-element.4) | data formatting | bytes 786432
  38.0 1.3 %copy.13 = f32[8,64]{1,0:T(8,128)} copy(f32[8,64]{1,0:T(8,128)} %get-tuple-element.5) | data formatting | bytes 4096

commit v2 on v1

--- a/solution.py
+++ b/solution.py
@@ -103,18 +103,34 @@
     half = 2 * atoms
     pairs = onehot.shape[1]
 
-    def target(d):
-        t = lax.rem(me + d, dev)
-        return t, {"qry": t // nl, "lib": lax.rem(t, nl)}
+    def wrap(x, n):
+        return jnp.where(x >= n, x - n, x)
+
+    near = [wrap(l + e, nl) for e in range(nl)]
+
+    def others(act):
+        for e in range(1, nl):
+            act(q * nl + near[e], q, near[e])
+
+        def step(d, carry):
+            tq = wrap(q + d, nq)
+            for e in range(nl):
+                act(tq * nl + near[e], tq, near[e])
+            return carry
+
+        lax.fori_loop(1, nq, step, 0)
+
+    def take(ref, sem):
+        pltpu.make_async_copy(ref, ref, sem).wait()
 
     barrier = pltpu.get_barrier_semaphore()
 
-    def greet(d, carry):
-        _, where = target(d)
-        pl.semaphore_signal(barrier, inc=1, device_id=where, device_id_type=pl.DeviceIdType.MESH)
-        return carry
-
-    lax.fori_loop(1, dev, greet, 0)
+    def greet(t, tq, tl):
+        pl.semaphore_signal(
+            barrier, inc=1, device_id={"qry": tq, "lib": tl}, device_id_type=pl.DeviceIdType.MESH
+        )
+
+    others(greet)
 
     lib_copy = pltpu.make_async_copy(lib_hbm, lib, loc_sem.at[0])
     conf_copy = pltpu.make_async_copy(conf_hbm, conf, loc_sem.at[1])
@@ -145,6 +161,53 @@
     owner_l = fdiv(owner, nq)
     owner_s = (owner - owner_l * nq) * nl + owner_l
 
+    pl.semaphore_wait(barrier, dev - 1)
+
+    def remote(src, dst, ssem, rsem, dq, dl):
+        return pltpu.make_async_remote_copy(
+            src_ref=src, dst_ref=dst, send_sem=ssem, recv_sem=rsem,
+            device_id={"qry": dq, "lib": dl}, device_id_type=pl.DeviceIdType.MESH,
+        )
+
+    def piece(bq, k):
+        return gath.at[k, pl.ds(pl.multiple_of(bq * block, block), block), :]
+
+    def stage1(d):
+        return remote(
+            qp_ref.at[:, pl.ds(pl.multiple_of(l * cols, cols), cols)], piece(q, l),
+            s1_send, s1_recv.at[d], lax.rem(z + d, nz) * CORES + c, l,
+        )
+
+    def from_z(d):
+        return lax.rem(z - d + nz, nz) * CORES + c
+
+    def stage2(d, e):
+        there = piece(from_z(d), l)
+        return remote(there, there, s2_send, s2_recv.at[d, e], q, lax.rem(l + e, nl))
+
+    def to_sib(bq, k):
+        there = piece(bq, k)
+        return remote(there, there, sib_send, sib_recv, sib, l)
+
+    def from_l(e):
+        return lax.rem(l - e + nl, nl)
+
+    for d in range(1, nz):
+        stage1(d).start()
+    for k in range(nl):
+        gath[k, pl.ds(pl.multiple_of(q * block, block), block), :] = qp_ref[:, k * cols : (k + 1) * cols]
+    for k in range(nl):
+        to_sib(q, k).start()
+
+    def pairwise(src, dst, ssem, rsem):
+        def start(t, tq, tl):
+            remote(src(t), dst, ssem, rsem, tq, tl).start()
+
+        return start
+
+    others(pairwise(lambda t: pack, atoms_in.at[me], at_send, at_recv))
+    atoms_in[me] = pack[...]
+
     owns = iota((dev, cand_n), 0) == owner_s
     owns_b = jnp.where(owns, 1.0, 0.0).astype(BF16)
     tri = jnp.where(iota((cand_n, cand_n), 0) < iota((cand_n, cand_n), 1), 1.0, 0.0).astype(BF16)
@@ -161,72 +224,11 @@
     for o in range(dev):
         bucket[o] = codes[o : o + 1]
 
-    pl.semaphore_wait(barrier, dev - 1)
-
-    def remote(src, dst, ssem, rsem, dq, dl):
-        return pltpu.make_async_remote_copy(
-            src_ref=src, dst_ref=dst, send_sem=ssem, recv_sem=rsem,
-            device_id={"qry": dq, "lib": dl}, device_id_type=pl.DeviceIdType.MESH,
-        )
-
-    def piece(bq, k):
-        return gath.at[k, pl.ds(pl.multiple_of(bq * block, block), block), :]
-
-    def stage1(d):
-        return remote(
-            qp_ref.at[:, pl.ds(pl.multiple_of(l * cols, cols), cols)], piece(q, l),
-            s1_send.at[d], s1_recv.at[d], lax.rem(z + d, nz) * CORES + c, l,
-        )
-
-    def from_z(d):
-        return lax.rem(z - d + nz, nz) * CORES + c
-
-    def stage2(d, e):
-        there = piece(from_z(d), l)
-        return remote(there, there, s2_send.at[d, e], s2_recv.at[d, e], q, lax.rem(l + e, nl))
-
-    def to_sib(bq, k, i, j):
-        there = piece(bq, k)
-        return remote(there, there, sib_send.at[i, j], sib_recv.at[i, j], sib, l)
-
-    def from_l(e):
-        return lax.rem(l - e + nl, nl)
-
-    def sib_block(d):
-        return lax.rem(z - d + nz, nz) * CORES + (1 - c)
-
-    for d in range(1, nz):
-        stage1(d).start()
-    for k in range(nl):
-        gath[k, pl.ds(pl.multiple_of(q * block, block), block), :] = qp_ref[:, k * cols : (k + 1) * cols]
-    for k in range(nl):
-        to_sib(q, k, 0, k).start()
-
-    def pairwise(src, dst, ssem, rsem):
-        def make(d):
-            t, where = target(d)
-            return pltpu.make_async_remote_copy(
-                src_ref=src(t), dst_ref=dst, send_sem=ssem.at[d], recv_sem=rsem.at[d],
-                device_id=where, device_id_type=pl.DeviceIdType.MESH,
-            )
-        return make
-
-    send_code = pairwise(lambda t: bucket.at[t], codes_in.at[me], co_send, co_recv)
-    send_atom = pairwise(lambda t: pack, atoms_in.at[me], at_send, at_recv)
-    send_back = pairwise(lambda t: ret_out.at[t], ret_in.at[me], re_send, re_recv)
-
-    def launch(d, carry):
-        send_code(d).start()
-        send_atom(d).start()
-        return carry
-
-    lax.fori_loop(1, dev, launch, 0)
+    others(pairwise(lambda t: bucket.at[t], codes_in.at[me], co_send, co_recv))
     codes_in[me] = bucket[me]
-    atoms_in[me] = pack[...]
 
     conf_copy.wait()
-    conf_t = jnp.transpose(conf[...])
-    comps = prepare(*(conf_t[i * atoms : (i + 1) * atoms] for i in range(4)))
+    comps = prepare(*(conf[i * atoms : (i + 1) * atoms] for i in range(4)))
     for i in range(4):
         confp[i * atoms : (i + 1) * atoms] = comps[i]
 
@@ -241,14 +243,11 @@
         stage1(d).wait_recv()
         for e in range(1, nl):
             stage2(d, e).start()
-        to_sib(from_z(d), l, d, 0).start()
-
-    def landed(d, carry):
-        send_code(d).wait_recv()
-        send_atom(d).wait_recv()
-        return carry
-
-    lax.fori_loop(1, dev, landed, 0)
+        to_sib(from_z(d), l).start()
+
+    rest = pl.ds(0, dev - 1)
+    take(codes_in.at[rest], co_recv)
+    take(atoms_in.at[rest], at_recv)
 
     got = codes_in[...].reshape(dev, LANES)
     pair_at = iota((1, pairs), 1)
@@ -303,19 +302,11 @@
     for d in range(1, nz):
         for e in range(1, nl):
             stage2(d, e).wait_recv()
-            to_sib(from_z(d), from_l(e), d, e).start()
+            to_sib(from_z(d), from_l(e)).start()
 
     lax.fori_loop(first, groups, cross_step, 0)
 
-    def sib_wait(bq, k, i, j):
-        to_sib(bq, k, i, j).wait_recv()
-
-    for k in range(nl):
-        sib_wait(sib, k, 0, k)
-    for d in range(1, nz):
-        sib_wait(sib_block(d), l, d, 0)
-        for e in range(1, nl):
-            sib_wait(sib_block(d), from_l(e), d, e)
+    take(gath.at[:, pl.ds(0, nz * block), :], sib_recv)
     lib_copy.wait()
 
     rows = nq * block
@@ -343,34 +334,15 @@
     for s in range(dev):
         ret_out[s] = back[s : s + 1]
 
-    def launch_back(d, carry):
-        send_back(d).start()
-        return carry
-
-    lax.fori_loop(1, dev, launch_back, 0)
+    others(pairwise(lambda t: ret_out.at[t], ret_in.at[me], re_send, re_recv))
     ret_in[me] = ret_out[me]
 
-    for d in range(1, nz):
-        stage1(d).wait_send()
-        to_sib(from_z(d), l, d, 0).wait_send()
-        for e in range(1, nl):
-            stage2(d, e).wait_send()
-            to_sib(from_z(d), from_l(e), d, e).wait_send()
-    for k in range(nl):
-        to_sib(q, k, 0, k).wait_send()
-
-    def settle(d, carry):
-        send_code(d).wait_send()
-        send_atom(d).wait_send()
-        return carry
-
-    lax.fori_loop(1, dev, settle, 0)
-
-    def landed_back(d, carry):
-        send_back(d).wait_recv()
-        return carry
-
-    lax.fori_loop(1, dev, landed_back, 0)
+    take(gath.at[0, pl.ds(0, (nz - 1) * block), :], s1_send)
+    take(gath.at[pl.ds(0, nl - 1), pl.ds(0, (nz - 1) * block), :], s2_send)
+    take(gath.at[:, pl.ds(0, nz * block), :], sib_send)
+    take(bucket.at[rest], co_send)
+    take(atoms_in.at[rest], at_send)
+    take(ret_in.at[rest], re_recv)
 
     came = jnp.transpose(ret_in[...].reshape(dev, LANES))
     hi_b, lo_b = split2(came)
@@ -381,11 +353,7 @@
         live = iota((1, listed), 1) < count_ref[i]
         out_ref[i : i + 1, :] = jnp.where(live, line, 0.0)
 
-    def settle_back(d, carry):
-        send_back(d).wait_send()
-        return carry
-
-    lax.fori_loop(1, dev, settle_back, 0)
+    take(ret_out.at[rest], re_send)
 
 
 def body(nq, nl, query_prints, library_prints, query_atoms, conformer_atoms, candidates, candidate_count, home_row):
@@ -400,6 +368,7 @@
     id_bytes = ((home_row.shape[0] - 1).bit_length() + 7) // 8
     rows = nq * block
     nz = nq // CORES
+    limit = (50 if dev <= 64 else 56) * 1024 * 1024
     vm = pltpu.VMEM
     dma = pltpu.SemaphoreType.DMA
     vspec = pl.BlockSpec(memory_space=pltpu.VMEM)
@@ -416,7 +385,7 @@
         out_specs=(vspec, vspec),
         scratch_shapes=[
             vm((own_rows, width), BF16),
-            vm((own_rows, 4 * atoms), F32),
+            vm((4 * atoms, own_rows), F32),
             vm((nl, rows, width // nl), BF16),
             vm((2 * local_q, LANES), BF16),
             vm((dev, 2 * local_q, LANES), BF16),
@@ -435,18 +404,18 @@
             vm((1, pairs), F32),
             vm((1, pairs), F32),
             dma((2,)),
-            dma((nz,)), dma((nz,)),
-            dma((nz, nl)), dma((nz, nl)),
-            dma((nz, nl)), dma((nz, nl)),
-            dma((dev,)), dma((dev,)),
-            dma((dev,)), dma((dev,)),
-            dma((dev,)), dma((dev,)),
+            dma, dma((nz,)),
+            dma, dma,
+            dma, dma((nz, nl)),
+            dma, dma,
+            dma, dma,
+            dma, dma,
         ],
         compiler_params=pltpu.CompilerParams(
-            collective_id=0, has_side_effects=True, vmem_limit_bytes=56 * 1024 * 1024
+            collective_id=0, has_side_effects=True, vmem_limit_bytes=limit
         ),
     )(
-        query_prints, library_prints, query_atoms, conformer_atoms, candidates, candidate_count,
+        query_prints, library_prints, query_atoms, conformer_atoms.T, candidates, candidate_count,
         home_row.reshape(-1, LANES),
     )
 

time: 39.5 us -> 36.8 us (0.932)
  Pallas kernels: 33.4 us -> 29.7 us
  local copies, waits for them, and re-layouts: 5.25 us -> 6.23 us
    pallas_call x1, Pallas kernels: 33.4 us -> 29.7 us  [body(): pl.pallas_call(functools.partial(kernel, nq, nl, cap, id_bytes), out_shap...]
    unnamed x3 -> x14, local copies, waits for them, and re-layouts: 5.25 us -> 6.23 us
where the time goes in v2:
time: 36.8 us; the launch traced here: 36.5 us
  Pallas kernels  29.7 us (81%)
  local copies, waits for them, and re-layouts  6.23 us (17%)
  between operations  0.65 us (2%)
    pallas_call x1, Pallas kernels, body(): pl.pallas_call(functools.partial(kernel, nq, nl, cap, id_bytes), out_shap...  29.7 us
    unnamed x14, local copies, waits for them, and re-layouts  6.23 us

profile of v2, /device:TPU:0, one launch (start us, length us, event | category | flops | bytes accessed | tf_op | source)
XLA Modules:
  0.0 36.5 jit_solution(64830211379742449)
XLA Ops:
  0.6 0.0 copy-start
  0.6 1.1 %copy-done = f32[768,192]{0,1:T(8,128)S(1)} copy-done((f32[768,192]{0,1:T(8,128)S(1)}, f32[768,192]{0,1:T(8,128)}, u32[]{:S(2)}) %copy-start) | copy-done | bytes 589848
  1.7 0.0 copy-start.1
  1.7 0.9 %copy-done.1 = bf16[32,2048]{1,0:T(8,128)(2,1)S(1)} copy-done((bf16[32,2048]{1,0:T(8,128)(2,1)S(1)}, bf16[32,2048]{1,0:T(8,128)(2,1)}, u32[]{:S(2)}) %copy-start.1) | copy-done | bytes 131096
  2.6 0.0 copy-start.2
  2.6 0.9 %copy-done.2 = s32[24576]{0:T(1024)S(1)} copy-done((s32[24576]{0:T(1024)S(1)}, s32[24576]{0:T(1024)}, u32[]{:S(2)}) %copy-start.2) | copy-done | bytes 98328
  3.5 0.0 copy-start.3
  3.5 0.7 %copy-done.3 = f32[8,192]{1,0:T(8,128)S(1)} copy-done((f32[8,192]{1,0:T(8,128)S(1)}, f32[8,192]{1,0:T(8,128)}, u32[]{:S(2)}) %copy-start.3) | copy-done | bytes 6168
  4.2 0.0 copy-start.4
  4.2 0.7 %copy-done.4 = s32[8,64]{1,0:T(8,128)S(1)} copy-done((s32[8,64]{1,0:T(8,128)S(1)}, s32[8,64]{1,0:T(8,128)}, u32[]{:S(2)}) %copy-start.4) | copy-done | bytes 2072
  4.9 0.0 copy-start.5
  4.9 0.7 %copy-done.5 = s32[8]{0:T(128)S(1)} copy-done((s32[8]{0:T(128)S(1)}, s32[8]{0:T(128)}, u32[]{:S(2)}) %copy-start.5) | copy-done | bytes 56
  5.5 29.7 %shard_map.86 = (bf16[256,768]{1,0:T(8,128)(2,1)S(1)}, f32[8,64]{1,0:T(8,128)S(1)}) custom-call(bf16[32,2048]{1,0:T(8,128)(2,1)S(1)} %copy-done.1, bf16[768,2048]{1,0:T(8,128)(2,1)} %lib_hbm.1, f32[8,192]{1,0:T(8,128)S(1)} %copy-done.3, f32[192,768]{1,0:T(8,128)S(1)} %bitcast.2, s32[8,64]{1,0:T(8,128)S(1)} %copy-done.4, s32[8]{0:T(128)S(1)} %copy-done.5, ...), custom_call_target="tpu_custom_call" | custom-call | tf_op jit(solution)/shard_map/pallas_call | solution.py:376
  35.2 0.7 %copy.11 = bf16[256,768]{1,0:T(8,128)(2,1)} copy(bf16[256,768]{1,0:T(8,128)(2,1)S(1)} %get-tuple-element.4) | data formatting | bytes 786432
  36.0 0.6 %copy.12 = f32[8,64]{1,0:T(8,128)} copy(f32[8,64]{1,0:T(8,128)S(1)} %get-tuple-element.5) | data formatting | bytes 4096
Async XLA Ops:
  0.6 1.1 %copy-start = (f32[768,192]{0,1:T(8,128)S(1)}, f32[768,192]{0,1:T(8,128)}, u32[]{:S(2)}) copy-start(f32[768,192]{0,1:T(8,128)} %param.10) | copy-start | bytes 1769476
  1.7 0.9 %copy-start.1 = (bf16[32,2048]{1,0:T(8,128)(2,1)S(1)}, bf16[32,2048]{1,0:T(8,128)(2,1)}, u32[]{:S(2)}) copy-start(bf16[32,2048]{1,0:T(8,128)(2,1)} %qp_ref.1) | copy-start | bytes 393220
  2.6 0.9 %copy-start.2 = (s32[24576]{0:T(1024)S(1)}, s32[24576]{0:T(1024)}, u32[]{:S(2)}) copy-start(s32[24576]{0:T(1024)} %param.13) | copy-start | bytes 294916
  3.5 0.7 %copy-start.3 = (f32[8,192]{1,0:T(8,128)S(1)}, f32[8,192]{1,0:T(8,128)}, u32[]{:S(2)}) copy-start(f32[8,192]{1,0:T(8,128)} %qa_ref.1) | copy-start | bytes 18436
  4.2 0.7 %copy-start.4 = (s32[8,64]{1,0:T(8,128)S(1)}, s32[8,64]{1,0:T(8,128)}, u32[]{:S(2)}) copy-start(s32[8,64]{1,0:T(8,128)} %cand_ref.1) | copy-start | bytes 6148
  4.9 0.7 %copy-start.5 = (s32[8]{0:T(128)S(1)}, s32[8]{0:T(128)}, u32[]{:S(2)}) copy-start(s32[8]{0:T(128)} %count_ref.1) | copy-start | bytes 100

commit v3 on v2

--- a/solution.py
+++ b/solution.py
@@ -80,12 +80,13 @@
 
 def kernel(
     nq, nl, cap, id_bytes,
-    qp_ref, lib_hbm, qa_ref, conf_hbm, cand_ref, count_ref, home_ref,
+    qp_hbm, lib_hbm, qa_hbm, conf_hbm, cand_hbm, count_hbm, home_hbm,
     tv_ref, out_ref,
-    lib, conf, gath, pack, atoms_in, bucket, codes_in, ret_out, ret_in,
+    qp_ref, qa_ref, cand_ref, count_ref, home_ref,
+    lib, conf, gath, pack, atoms_in, bucket, mid, codes_in, ret_out, mid_back, ret_in,
     confp, qprep, pairs_c, pairs_q, onehot, qonehot, cself, qself, shape_s, valid_s,
     loc_sem, s1_send, s1_recv, sib_send, sib_recv, s2_send, s2_recv,
-    at_send, at_recv, co_send, co_recv, re_send, re_recv,
+    send_a, recv_a, send_b, recv_b,
 ):
     q = lax.axis_index("qry")
     l = lax.axis_index("lib")
@@ -106,36 +107,34 @@
     def wrap(x, n):
         return jnp.where(x >= n, x - n, x)
 
-    near = [wrap(l + e, nl) for e in range(nl)]
-
-    def others(act):
-        for e in range(1, nl):
-            act(q * nl + near[e], q, near[e])
-
-        def step(d, carry):
-            tq = wrap(q + d, nq)
-            for e in range(nl):
-                act(tq * nl + near[e], tq, near[e])
-            return carry
-
-        lax.fori_loop(1, nq, step, 0)
+    lib_peers = [wrap(l + e, nl) for e in range(1, nl)]
+    qry_peers = [wrap(q + d, nq) for d in range(1, nq)]
 
     def take(ref, sem):
         pltpu.make_async_copy(ref, ref, sem).wait()
 
     barrier = pltpu.get_barrier_semaphore()
 
-    def greet(t, tq, tl):
+    for tq, tl in [(q, t) for t in lib_peers] + [(t, l) for t in qry_peers]:
         pl.semaphore_signal(
             barrier, inc=1, device_id={"qry": tq, "lib": tl}, device_id_type=pl.DeviceIdType.MESH
         )
 
-    others(greet)
-
+    loads = [
+        pltpu.make_async_copy(src, dst, loc_sem.at[2 + n])
+        for n, (src, dst) in enumerate(
+            ((qa_hbm, qa_ref), (cand_hbm, cand_ref), (home_hbm, home_ref), (qp_hbm, qp_ref), (count_hbm, count_ref))
+        )
+    ]
+    for load in loads:
+        load.start()
     lib_copy = pltpu.make_async_copy(lib_hbm, lib, loc_sem.at[0])
     conf_copy = pltpu.make_async_copy(conf_hbm, conf, loc_sem.at[1])
     conf_copy.start()
     lib_copy.start()
+
+    for load in loads:
+        load.wait()
 
     qa = qa_ref[...]
     zero = jnp.zeros((local_q, LANES - half), F32)
@@ -158,10 +157,8 @@
         stored = stored + (byte.astype(I32) << (8 * k))
     owner = fdiv(stored, own_rows)
     slot = stored - owner * own_rows
-    owner_l = fdiv(owner, nq)
-    owner_s = (owner - owner_l * nq) * nl + owner_l
-
-    pl.semaphore_wait(barrier, dev - 1)
+
+    pl.semaphore_wait(barrier, nq + nl - 2)
 
     def remote(src, dst, ssem, rsem, dq, dl):
         return pltpu.make_async_remote_copy(
@@ -199,16 +196,11 @@
     for k in range(nl):
         to_sib(q, k).start()
 
-    def pairwise(src, dst, ssem, rsem):
-        def start(t, tq, tl):
-            remote(src(t), dst, ssem, rsem, tq, tl).start()
-
-        return start
-
-    others(pairwise(lambda t: pack, atoms_in.at[me], at_send, at_recv))
-    atoms_in[me] = pack[...]
-
-    owns = iota((dev, cand_n), 0) == owner_s
+    for t in qry_peers:
+        remote(pack, atoms_in.at[q, l], send_a.at[0], recv_a.at[0], t, l).start()
+    atoms_in[q, l] = pack[...]
+
+    owns = iota((dev, cand_n), 0) == owner
     owns_b = jnp.where(owns, 1.0, 0.0).astype(BF16)
     tri = jnp.where(iota((cand_n, cand_n), 0) < iota((cand_n, cand_n), 1), 1.0, 0.0).astype(BF16)
     before = nn(owns_b, tri)
@@ -222,15 +214,27 @@
     sums = nt(left, rank_b).astype(I32)
     codes = sums[:dev] + (sums[dev:] << 7)
     for o in range(dev):
-        bucket[o] = codes[o : o + 1]
-
-    others(pairwise(lambda t: bucket.at[t], codes_in.at[me], co_send, co_recv))
-    codes_in[me] = bucket[me]
+        bucket[o // nq, o % nq] = codes[o : o + 1]
+
+    for t in lib_peers:
+        remote(bucket.at[t], mid.at[l], send_a.at[1], recv_a.at[1], q, t).start()
+    mid[l] = bucket[l]
 
     conf_copy.wait()
     comps = prepare(*(conf[i * atoms : (i + 1) * atoms] for i in range(4)))
     for i in range(4):
         confp[i * atoms : (i + 1) * atoms] = comps[i]
+
+    q_rest = pl.ds(0, nq - 1)
+    l_rest = pl.ds(0, nl - 1)
+    take(atoms_in.at[q_rest, 0], recv_a.at[0])
+    for t in lib_peers:
+        remote(atoms_in.at[:, l], atoms_in.at[:, l], send_b.at[0], recv_b.at[0], q, t).start()
+    take(mid.at[l_rest], recv_a.at[1])
+    for t in qry_peers:
+        remote(mid.at[:, t], codes_in.at[q], send_b.at[1], recv_b.at[1], t, l).start()
+    for k in range(nl):
+        codes_in[q, k] = mid[k, q]
 
     def self_step(g, carry):
         lanes = pl.ds(pl.multiple_of(g * LANES, LANES), LANES)
@@ -245,9 +249,8 @@
             stage2(d, e).start()
         to_sib(from_z(d), l).start()
 
-    rest = pl.ds(0, dev - 1)
-    take(codes_in.at[rest], co_recv)
-    take(atoms_in.at[rest], at_recv)
+    take(codes_in.at[q_rest], recv_b.at[1])
+    take(atoms_in.at[:, l_rest], recv_b.at[0])
 
     got = codes_in[...].reshape(dev, LANES)
     pair_at = iota((1, pairs), 1)
@@ -267,7 +270,7 @@
     onehot[...] = jnp.where(iota((own_rows, pairs), 0) == pslot, 1.0, 0.0).astype(BF16)
     qonehot[...] = jnp.where(iota((dev * local_q, pairs), 0) == pquery, 1.0, 0.0).astype(BF16)
 
-    raw = atoms_in[...].astype(F32)
+    raw = atoms_in[...].reshape(dev, 2 * local_q, LANES).astype(F32)
     q_top = jnp.transpose(raw[:, :local_q].reshape(dev * local_q, LANES))
     q_low = jnp.transpose(raw[:, local_q:].reshape(dev * local_q, LANES))
     comps = prepare(q_top[:atoms], q_top[atoms:half], q_low[:atoms], q_low[atoms:half])
@@ -332,17 +335,26 @@
     hi_s, lo_s = split2(jnp.where(src_hot, score, 0.0))
     back = nt(hi_s, j_hot) + nt(lo_s, j_hot)
     for s in range(dev):
-        ret_out[s] = back[s : s + 1]
-
-    others(pairwise(lambda t: ret_out.at[t], ret_in.at[me], re_send, re_recv))
-    ret_in[me] = ret_out[me]
+        ret_out[s // nl, s % nl] = back[s : s + 1]
+
+    for t in qry_peers:
+        remote(ret_out.at[t], mid_back.at[q], send_a.at[2], recv_a.at[2], t, l).start()
+    mid_back[q] = ret_out[q]
+    take(mid_back.at[q_rest], recv_a.at[2])
+    for t in lib_peers:
+        remote(mid_back.at[:, t], ret_in.at[l], send_b.at[2], recv_b.at[2], q, t).start()
+    for k in range(nq):
+        ret_in[l, k] = mid_back[k, l]
 
     take(gath.at[0, pl.ds(0, (nz - 1) * block), :], s1_send)
     take(gath.at[pl.ds(0, nl - 1), pl.ds(0, (nz - 1) * block), :], s2_send)
     take(gath.at[:, pl.ds(0, nz * block), :], sib_send)
-    take(bucket.at[rest], co_send)
-    take(atoms_in.at[rest], at_send)
-    take(ret_in.at[rest], re_recv)
+    take(atoms_in.at[q_rest, 0], send_a.at[0])
+    take(mid.at[l_rest], send_a.at[1])
+    take(mid_back.at[q_rest], send_a.at[2])
+    take(atoms_in.at[:, l_rest], send_b.at[0])
+    take(codes_in.at[q_rest], send_b.at[1])
+    take(ret_in.at[l_rest], recv_b.at[2])
 
     came = jnp.transpose(ret_in[...].reshape(dev, LANES))
     hi_b, lo_b = split2(came)
@@ -353,7 +365,7 @@
         live = iota((1, listed), 1) < count_ref[i]
         out_ref[i : i + 1, :] = jnp.where(live, line, 0.0)
 
-    take(ret_out.at[rest], re_send)
+    take(ret_in.at[l_rest], send_b.at[2])
 
 
 def body(nq, nl, query_prints, library_prints, query_atoms, conformer_atoms, candidates, candidate_count, home_row):
@@ -368,31 +380,35 @@
     id_bytes = ((home_row.shape[0] - 1).bit_length() + 7) // 8
     rows = nq * block
     nz = nq // CORES
-    limit = (50 if dev <= 64 else 56) * 1024 * 1024
+    limit = 56 * 1024 * 1024
     vm = pltpu.VMEM
     dma = pltpu.SemaphoreType.DMA
     vspec = pl.BlockSpec(memory_space=pltpu.VMEM)
-    aspec = pl.BlockSpec(memory_space=pl.ANY)
     return pl.pallas_call(
         functools.partial(kernel, nq, nl, cap, id_bytes),
         out_shape=(
             jax.ShapeDtypeStruct((rows, own_rows), BF16),
             jax.ShapeDtypeStruct((local_q, listed), F32),
         ),
-        in_specs=[
-            vspec, aspec, vspec, aspec, vspec, pl.BlockSpec(memory_space=pltpu.SMEM), vspec,
-        ],
+        in_specs=[pl.BlockSpec(memory_space=pltpu.HBM)] * 7,
         out_specs=(vspec, vspec),
         scratch_shapes=[
+            vm((block, width), BF16),
+            vm((local_q, 4 * atoms), F32),
+            vm((local_q, listed), I32),
+            pltpu.SMEM((local_q,), I32),
+            vm((home_row.shape[0] // LANES, LANES), I32),
             vm((own_rows, width), BF16),
             vm((4 * atoms, own_rows), F32),
             vm((nl, rows, width // nl), BF16),
             vm((2 * local_q, LANES), BF16),
-            vm((dev, 2 * local_q, LANES), BF16),
-            vm((dev, 1, LANES), I32),
-            vm((dev, 1, LANES), I32),
-            vm((dev, 1, LANES), F32),
-            vm((dev, 1, LANES), F32),
+            vm((nq, nl, 2 * local_q, LANES), BF16),
+            vm((nl, nq, 1, LANES), I32),
+            vm((nl, nq, 1, LANES), I32),
+            vm((nq, nl, 1, LANES), I32),
+            vm((nq, nl, 1, LANES), F32),
+            vm((nq, nl, 1, LANES), F32),
+            vm((nl, nq, 1, LANES), F32),
             vm((4 * atoms, own_rows), F32),
             vm((4 * atoms, rows), F32),
             vm((4 * atoms + 8, pairs), F32),
@@ -403,13 +419,12 @@
             vm((1, rows), F32),
             vm((1, pairs), F32),
             vm((1, pairs), F32),
-            dma((2,)),
+            dma((7,)),
             dma, dma((nz,)),
             dma, dma,
             dma, dma((nz, nl)),
-            dma, dma,
-            dma, dma,
-            dma, dma,
+            dma((3,)), dma((3,)),
+            dma((3,)), dma((3,)),
         ],
         compiler_params=pltpu.CompilerParams(
             collective_id=0, has_side_effects=True, vmem_limit_bytes=limit

time: 36.8 us -> 35.2 us (0.957)
  local copies, waits for them, and re-layouts: 6.23 us -> 3.03 us
  Pallas kernels: 29.7 us -> 31.3 us
    unnamed x14 -> x2, local copies, waits for them, and re-layouts: 6.23 us -> 3.03 us
    pallas_call x1, Pallas kernels: 29.7 us -> 31.3 us  [body(): pl.pallas_call(functools.partial(kernel, nq, nl, cap, id_bytes), out_shap...]
where the time goes in v3:
time: 35.2 us; the launch traced here: 35 us
  Pallas kernels  31.3 us (89%)
  local copies, waits for them, and re-layouts  3.03 us (9%)
  between operations  0.64 us (2%)
    pallas_call x1, Pallas kernels, body(): pl.pallas_call(functools.partial(kernel, nq, nl, cap, id_bytes), out_shap...  31.3 us
    unnamed x2, local copies, waits for them, and re-layouts  3.03 us

profile of v3, /device:TPU:0, one launch (start us, length us, event | category | flops | bytes accessed | tf_op | source)
XLA Modules:
  0.0 35.0 jit_solution(13860067340454442644)
XLA Ops:
  0.6 31.3 %shard_map.86 = (bf16[256,768]{1,0:T(8,128)(2,1)}, f32[8,64]{1,0:T(8,128)}) custom-call(bf16[32,2048]{1,0:T(8,128)(2,1)} %qp_hbm.1, bf16[768,2048]{1,0:T(8,128)(2,1)} %lib_hbm.1, f32[8,192]{1,0:T(8,128)} %qa_hbm.1, f32[192,768]{1,0:T(8,128)} %bitcast.2, s32[8,64]{1,0:T(8,128)} %cand_hbm.1, s32[8]{0:T(128)} %count_hbm.1, s32[192,128]{1,0:T(8,128)} %bitcast.3), custom_call_target="tpu_custom_call" | custom-call | tf_op jit(solution)/shard_map/pallas_call | solution.py:387
  31.9 1.8 %copy.11 = bf16[256,768]{1,0:T(8,128)(2,1)} copy(bf16[256,768]{1,0:T(8,128)(2,1)} %get-tuple-element.4) | data formatting | bytes 786432
  33.7 1.3 %copy.12 = f32[8,64]{1,0:T(8,128)} copy(f32[8,64]{1,0:T(8,128)} %get-tuple-element.5) | data formatting | bytes 4096

commit v4 on v3

--- a/solution.py
+++ b/solution.py
@@ -81,7 +81,8 @@
 def kernel(
     nq, nl, cap, id_bytes,
     qp_hbm, lib_hbm, qa_hbm, conf_hbm, cand_hbm, count_hbm, home_hbm,
-    tv_ref, out_ref,
+    tv_hbm, out_ref,
+    tv_ref,
     qp_ref, qa_ref, cand_ref, count_ref, home_ref,
     lib, conf, gath, pack, atoms_in, bucket, mid, codes_in, ret_out, mid_back, ret_in,
     confp, qprep, pairs_c, pairs_q, onehot, qonehot, cself, qself, shape_s, valid_s,
@@ -325,12 +326,14 @@
             sq = jnp.sum(wide * wide, axis=1, keepdims=True)
             scores = prod if scores is None else scores + prod
             norms = sq if norms is None else norms + sq
-        tv = (scores / (norms + EPSILON)).astype(BF16)
+        tv = (scores * (1.0 / (norms + EPSILON))).astype(BF16)
         tv_ref[r : r + chunk, :] = tv
         chosen = nn(tv, onehot[...]) * qonehot[r : r + chunk, :].astype(F32)
         chosen = jnp.sum(chosen, axis=0, keepdims=True)
         priors = chosen if priors is None else priors + chosen
 
+    tv_copy = pltpu.make_async_copy(tv_ref, tv_hbm, loc_sem.at[7])
+    tv_copy.start()
     score = jnp.where(valid_s[...] > 0.0, shape_s[...] + priors, 0.0)
     hi_s, lo_s = split2(jnp.where(src_hot, score, 0.0))
     back = nt(hi_s, j_hot) + nt(lo_s, j_hot)
@@ -366,6 +369,7 @@
         out_ref[i : i + 1, :] = jnp.where(live, line, 0.0)
 
     take(ret_in.at[l_rest], send_b.at[2])
+    tv_copy.wait()
 
 
 def body(nq, nl, query_prints, library_prints, query_atoms, conformer_atoms, candidates, candidate_count, home_row):
@@ -391,8 +395,9 @@
             jax.ShapeDtypeStruct((local_q, listed), F32),
         ),
         in_specs=[pl.BlockSpec(memory_space=pltpu.HBM)] * 7,
-        out_specs=(vspec, vspec),
+        out_specs=(pl.BlockSpec(memory_space=pl.ANY), vspec),
         scratch_shapes=[
+            vm((rows, own_rows), BF16),
             vm((block, width), BF16),
             vm((local_q, 4 * atoms), F32),
             vm((local_q, listed), I32),
@@ -419,7 +424,7 @@
             vm((1, rows), F32),
             vm((1, pairs), F32),
             vm((1, pairs), F32),
-            dma((7,)),
+            dma((8,)),
             dma, dma((nz,)),
             dma, dma,
             dma, dma((nz, nl)),

time: 35.2 us -> 35.1 us (level)
  no operation moved by 1% of the time
where the time goes in v4:
time: 35.1 us; the launch traced here: 34.8 us
  Pallas kernels  31.1 us (89%)
  local copies, waits for them, and re-layouts  3.03 us (9%)
  between operations  0.64 us (2%)
    pallas_call x1, Pallas kernels, body(): pl.pallas_call(functools.partial(kernel, nq, nl, cap, id_bytes), out_shap...  31.1 us
    unnamed x2, local copies, waits for them, and re-layouts  3.03 us

profile of v4, /device:TPU:0, one launch (start us, length us, event | category | flops | bytes accessed | tf_op | source)
XLA Modules:
  0.0 34.8 jit_solution(13599801158474610621)
XLA Ops:
  0.6 31.1 %shard_map.86 = (bf16[256,768]{1,0:T(8,128)(2,1)}, f32[8,64]{1,0:T(8,128)}) custom-call(bf16[32,2048]{1,0:T(8,128)(2,1)} %qp_hbm.1, bf16[768,2048]{1,0:T(8,128)(2,1)} %lib_hbm.1, f32[8,192]{1,0:T(8,128)} %qa_hbm.1, f32[192,768]{1,0:T(8,128)} %bitcast.2, s32[8,64]{1,0:T(8,128)} %cand_hbm.1, s32[8]{0:T(128)} %count_hbm.1, s32[192,128]{1,0:T(8,128)} %bitcast.3), custom_call_target="tpu_custom_call" | custom-call | tf_op jit(solution)/shard_map/pallas_call | solution.py:391
  31.8 1.8 %copy.11 = bf16[256,768]{1,0:T(8,128)(2,1)} copy(bf16[256,768]{1,0:T(8,128)(2,1)} %get-tuple-element.4) | data formatting | bytes 786432
  33.6 1.3 %copy.12 = f32[8,64]{1,0:T(8,128)} copy(f32[8,64]{1,0:T(8,128)} %get-tuple-element.5) | data formatting | bytes 4096
